TPU v7x, 128 devices: a whole 4x4x4 slice. The times are simulated.
128 devices in a mesh: dp: 16 (over z, y), expert: 8 (over x, core).
Axes of the slice: x: 4, y: 4, z: 4, core: 2. Of those that a mesh axis runs over, the one named last changes fastest.
Arguments:
- inputs: bfloat16 [8192, 2048], P('dp', 'expert'), may hold values from -6 to 6
- grad_output: bfloat16 [8192, 2048], P('dp', 'expert'), may hold values from -6 to 6
- gates: bfloat16 [8192, 8], P('dp'), may hold values from 0.019897461 to 0.3984375
- expert_ids: int32 [8192, 8], P('dp'), may hold values from 0 to 127, all different within a row; in each aligned block of 512 rows (0 to 511, 512 to 1023, ...) at most 64 rows name the same one
- owner: int32 [128], replicated, may hold values from 0 to 127, each once
- w_gate: bfloat16 [128, 2048, 768], P(('dp', 'expert')), may hold values from -0.125 to 0.125
- w_up: bfloat16 [128, 2048, 768], P(('dp', 'expert')), may hold values from -0.125 to 0.125
- w_down: bfloat16 [128, 768, 2048], P(('dp', 'expert')), may hold values from -0.21875 to 0.21875
Outputs:
- grad_inputs: bfloat16 [8192, 2048], P('dp', 'expert')
- grad_gates: bfloat16 [8192, 8], P('dp')
- grad_w_gate: bfloat16 [128, 2048, 768], P(('dp', 'expert'))
- grad_w_up: bfloat16 [128, 2048, 768], P(('dp', 'expert'))
- grad_w_down: bfloat16 [128, 768, 2048], P(('dp', 'expert'))
Inputs may be any that keep to these rules, and one draw needn't show every extreme that they name: `expert_ids`: in each aligned block of 512 tokens no expert is named by more than 64 slots, and in some block one expert is named by exactly 64; a token names 8 different experts. `owner`: each storage slot holds exactly one expert; slot s lies on the device of index s along dp+expert.
All inputs are finite; a program needn't handle non-finite values.
Results may differ from a plain program's by a relative error of at most 0.012.
Values may be sent and summed in bfloat16 or wider, within the bound.
A program may use at most 128 MiB of HBM per device.

v0:
```python
import jax
import jax.numpy as jnp
from jax import lax
from jax.experimental import pallas as pl
from jax.experimental.pallas import tpu as pltpu
from jax.sharding import PartitionSpec as P

D, FF, TOP, TOK, CAP = 2048, 768, 8, 512, 64
HALF = CAP // 2
SH = 256
WIDE = D + 128
SLOTS = 1024
SEMS = 160
BF, F32 = jnp.bfloat16, jnp.float32
MESH = pl.DeviceIdType.MESH
ORDER = (1, 3, 2)


def dot(left, right, dim_left, dim_right):
    return lax.dot_general(
        left, right, (((dim_left,), (dim_right,)), ((), ())), preferred_element_type=F32
    )


def iota(shape, dim):
    return lax.broadcasted_iota(jnp.int32, shape, dim).astype(F32)


def kernel(
    inp, gro, ids, gates, owner, wg_in, wu_in, wd_in,
    out_in, out_gates, out_wg, out_wu, out_wd,
    xin, ag, slots, gpack, grecv, pack, st1, st2, fin, wg, wu, wd, dz, act, dhg, dhu,
    bst1, bst2, back, pmat, tri, rall, onehot, core_in, rs_in, gsend, grecv_gates,
    send_sem, recv_sem, local_sem,
):
    row, col = lax.axis_index("dp"), lax.axis_index("expert")
    z, y = row // 4, row % 4
    x, c = col // 2, col % 2
    counts = {"remote": 0, "local": 0}

    def at(k, base):
        return (base + k + 4) % 4

    def zdev(k):
        return (at(k, z) * 4 + y, col)

    def ydev(k):
        return (z * 4 + at(k, y), col)

    def xdev(k, flip):
        return (row, at(k, x) * 2 + (c + flip) % 2)

    def send(src, dst, device):
        n = counts["remote"]
        counts["remote"] = n + 1
        copy = pltpu.make_async_remote_copy(
            src_ref=src, dst_ref=dst, send_sem=send_sem.at[n], recv_sem=recv_sem.at[n],
            device_id=device, device_id_type=MESH,
        )
        copy.start()
        return copy

    def local(src, dst):
        n = counts["local"]
        counts["local"] = n + 1
        copy = pltpu.make_async_copy(src, dst, local_sem.at[n])
        copy.start()
        return copy

    weights = [local(wg_in, wg), local(wu_in, wu), local(wd_in, wd)]
    own_in, own_gro = local(inp, xin.at[col]), local(gro, ag.at[row])

    barrier = pltpu.get_barrier_semaphore()
    peers = [zdev(k) for k in ORDER] + [ydev(k) for k in ORDER]
    peers += [xdev(k, f) for k in range(4) for f in range(2) if (k, f) != (0, 0)]
    for peer in peers:
        pl.semaphore_signal(barrier, inc=1, device_id=peer, device_id_type=MESH)
    pl.semaphore_wait(barrier, len(peers))

    x_own = [send(inp, xin.at[col], xdev(k, 0)) for k in ORDER]
    x_core = [send(inp, xin.at[col], xdev(0, 1))]
    lower, upper = pl.ds(0, TOK // 2), pl.ds(TOK // 2, TOK // 2)
    a_one = [send(gro.at[lower], ag.at[row, lower], ydev(k)) for k in ORDER]
    b_one = [send(gro.at[upper], ag.at[row, upper], zdev(k)) for k in ORDER]
    a_two = {0: [send(gro.at[lower], ag.at[row, lower], zdev(k)) for k in ORDER]}
    b_two = {0: [send(gro.at[upper], ag.at[row, upper], ydev(k)) for k in ORDER]}

    tri[...] = (iota((TOK, TOK), 0) <= iota((TOK, TOK), 1)).astype(BF)
    expert_no = lax.broadcasted_iota(jnp.int32, (128, TOK), 0)
    owner_row = jnp.broadcast_to(owner[...].astype(F32), (8, 128)).astype(BF)
    for k in range(TOP):
        match = (ids[k : k + 1, :] == expert_no).astype(F32).astype(BF)
        slots[row, k : k + 1, :] = dot(owner_row, match, 1, 0)[0:1, :]
    s_one = [send(slots.at[row], slots.at[row], ydev(k)) for k in ORDER]

    mine = slots[row]
    name = iota((16, TOK), 0) * 8.0 + col.astype(F32)
    member = jnp.zeros((16, TOK), F32)
    gate_of = jnp.zeros((16, TOK), F32)
    for k in range(TOP):
        hit = mine[k : k + 1, :] == name
        member += jnp.where(hit, 1.0, 0.0)
        gate_of += jnp.where(hit, gates[k : k + 1, :].astype(F32), 0.0)
    rank = dot(member.astype(BF), tri[...], 1, 0) * member
    place = iota((CAP, TOK), 0) + 1.0
    for d in range(16):
        hot = jnp.where(rank[d : d + 1, :] == place, 1.0, 0.0)
        pmat[d * CAP : (d + 1) * CAP, :] = hot.astype(BF)
        gate_col = jnp.sum(hot * gate_of[d : d + 1, :], axis=1, keepdims=True)
        pack[d // 4, d % 4, :, D:WIDE] = jnp.broadcast_to(gate_col, (CAP, 128)).astype(BF)

    for copy in s_one:
        copy.wait_recv()
    s_two = [
        send(slots.at[pl.ds(z * 4, 4)], slots.at[pl.ds(z * 4, 4)], zdev(k)) for k in ORDER
    ]
    for n, k in enumerate(ORDER):
        x_own[n].wait_recv()
        source = at(-k, x) * 2 + c
        x_core.append(send(xin.at[source], xin.at[source], xdev(0, 1)))
        a_one[n].wait_recv()
        source = z * 4 + at(-k, y)
        a_two[k] = [
            send(ag.at[source, lower], ag.at[source, lower], zdev(m)) for m in ORDER
        ]
        b_one[n].wait_recv()
        source = at(-k, z) * 4 + y
        b_two[k] = [
            send(ag.at[source, upper], ag.at[source, upper], ydev(m)) for m in ORDER
        ]

    for copy in x_core:
        copy.wait_recv()
    own_in.wait()

    def pack_inputs(shard, _):
        rows = dot(pmat[...], xin[shard], 1, 0).astype(BF)
        pack[:, :, :, pl.ds(pl.multiple_of(shard * SH, SH), SH)] = rows.reshape(4, 4, CAP, SH)
        return 0

    lax.fori_loop(0, 8, pack_inputs, 0)

    first, second = pl.ds(0, HALF), pl.ds(HALF, HALF)
    p_one = [send(pack.at[:, at(k, y), first], st1.at[y], ydev(k)) for k in ORDER]
    q_one = [send(pack.at[at(k, z), :, second], st2.at[z], zdev(k)) for k in ORDER]
    p_two = {0: [send(pack.at[at(k, z), y, first], fin.at[z, y, first], zdev(k)) for k in ORDER]}
    q_two = {0: [send(pack.at[z, at(k, y), second], fin.at[z, y, second], ydev(k)) for k in ORDER]}
    own_rows = [local(pack.at[z, y], fin.at[z, y])]

    for copy in s_two:
        copy.wait_recv()
    own_gro.wait()
    near = iota((8, TOK), 0) + row.astype(F32) * 8.0

    def find_members(r, _):
        found = jnp.zeros((8, TOK), F32)
        theirs = slots[r]
        for k in range(TOP):
            found += jnp.where(theirs[k : k + 1, :] == near, 1.0, 0.0)
        rall[pl.ds(pl.multiple_of(r * 8, 8), 8), :] = found
        return 0

    lax.fori_loop(0, 16, find_members, 0)
    rall[...] = dot(rall[...].astype(BF), tri[...], 1, 0) * rall[...]

    def pack_gradients(group):
        def one(step, _):
            r = group * 4 + step
            ranks = rall[pl.ds(pl.multiple_of(r * 8, 8), 8), :]
            for e in range(8):
                hot = jnp.where(ranks[e : e + 1, :] == place, 1.0, 0.0)
                onehot[e * CAP : (e + 1) * CAP, :] = hot.astype(BF)
            rows = dot(onehot[...], ag[r], 1, 0).astype(BF)
            gpack[:, group, step] = rows.reshape(8, CAP, SH)
            return 0

        lax.fori_loop(0, 4, one, 0)

    g_sent = {}
    own_grads = []

    def exchange_gradients(group, k):
        for m in (0, 1, 3, 2):
            for f in range(2):
                target = at(m, x) * 2 + (c + f) % 2
                if (m, f) == (0, 0):
                    own_grads.append(local(gpack.at[col, group], grecv.at[col, group]))
                else:
                    g_sent[k, m, f] = send(
                        gpack.at[target, group], grecv.at[col, group], xdev(m, f)
                    )

    for k in (0, 1, 3, 2):
        if k == 0:
            for copy in b_two[0]:
                copy.wait_recv()
        else:
            b_seen = b_two[k]
            for copy in b_seen:
                copy.wait_recv()
            n = ORDER.index(k)
            for source in (0, 1, 3, 2):
                a_two[source][n].wait_recv()
        group = at(-k, z)
        pack_gradients(group)
        exchange_gradients(group, k)

    for n, k in enumerate(ORDER):
        p_one[n].wait_recv()
        source = at(-k, y)
        p_two[k] = [
            send(st1.at[source, at(m, z)], fin.at[z, source, first], zdev(m)) for m in ORDER
        ]
        own_rows.append(local(st1.at[source, z], fin.at[z, source, first]))
        q_one[n].wait_recv()
        source = at(-k, z)
        q_two[k] = [
            send(st2.at[source, at(m, y)], fin.at[source, y, second], ydev(m)) for m in ORDER
        ]
        own_rows.append(local(st2.at[source, y], fin.at[source, y, second]))

    for copy in weights:
        copy.wait()
    for copy in own_grads:
        copy.wait()

    def add_dz(shard, start):
        columns = pl.ds(pl.multiple_of(shard * SH, SH), SH)

        def chunk(n, _):
            rows = pl.ds(pl.multiple_of(n * 256, 256), 256)
            part = dot(grecv[shard, n].reshape(256, SH), wd[:, columns], 1, 1)
            dz[rows, :] = part if start else dz[rows, :] + part
            return 0

        lax.fori_loop(0, 4, chunk, 0)

    add_dz(col, True)
    for m in (0, 1, 3, 2):
        for f in range(2):
            if (m, f) != (0, 0):
                for k in (0, 1, 3, 2):
                    g_sent[k, m, f].wait_recv()
                add_dz(at(-m, x) * 2 + (c + f) % 2, False)

    for copy in p_one + q_one + p_two[0] + q_two[0]:
        copy.wait_send()
    for k in (0,) + ORDER:
        for copy in p_two[k] + q_two[k]:
            copy.wait_recv()
    for copy in own_rows:
        copy.wait()

    def through_expert(group):
        rows = fin[group].reshape(256, WIDE)
        gate_col = rows[:, D : D + 1].astype(F32)
        h1 = dot(rows[:, :D], wg[...], 1, 0)
        h2 = dot(rows[:, :D], wu[...], 1, 0)
        here = pl.ds(pl.multiple_of(group * 256, 256), 256)
        dz_here = dz[here, :]
        sigma = jax.nn.sigmoid(h1)
        silu = h1 * sigma
        slope = sigma * (1.0 + h1 * (1.0 - sigma))
        acted = (silu * h2).astype(BF)
        act[here, :] = acted
        gate_grad = jnp.sum(acted.astype(F32) * dz_here, axis=1, keepdims=True)
        pack[group, :, :, D:WIDE] = (
            jnp.broadcast_to(gate_grad, (256, 128)).astype(BF).reshape(4, CAP, 128)
        )
        dfa = gate_col * dz_here
        dhg[here, :] = (dfa * h2 * slope).astype(BF)
        dhu[here, :] = (dfa * silu).astype(BF)

        def back_part(n, _):
            some = pl.ds(pl.multiple_of(n * 512, 512), 512)
            part = dot(dhg[here, :], wg[some, :], 1, 1) + dot(dhu[here, :], wu[some, :], 1, 1)
            pack[group, :, :, some] = part.astype(BF).reshape(4, CAP, 512)
            return 0

        lax.fori_loop(0, 4, back_part, 0)

    r_one, t_one, r_two, t_two, own_back = {}, {}, {}, {}, []

    def forward_back(step):
        if step < 3:
            r_one[step].wait_recv()
            source = at(-1 - step, z)
            r_two[step] = [
                send(bst1.at[source, at(m, y)], back.at[source, y, first], ydev(m)) for m in ORDER
            ]
            own_back.append(local(bst1.at[source, y], back.at[source, y, first]))
        target = at(1 + step, z)
        for n, k in enumerate(ORDER):
            t_one[step][n].wait_recv()
            source = at(-k, y)
            if step < 3:
                t_two[step].append(
                    send(bst2.at[source, target], back.at[z, source, second], zdev(1 + step))
                )
            else:
                own_back.append(local(bst2.at[source, z], back.at[z, source, second]))

    for step in range(4):
        group = at(1 + step, z)
        through_expert(group)
        if step < 3:
            r_one[step] = send(pack.at[group, :, first], bst1.at[z], zdev(1 + step))
            t_two[step] = [send(pack.at[group, y, second], back.at[z, y, second], zdev(1 + step))]
        else:
            r_two[step] = [
                send(pack.at[z, at(m, y), first], back.at[z, y, first], ydev(m)) for m in ORDER
            ]
            own_back.append(local(pack.at[z, y], back.at[z, y]))
        t_one[step] = [
            send(pack.at[group, at(m, y), second], bst2.at[y, group], ydev(m)) for m in ORDER
        ]
        if step >= 2:
            forward_back(step - 2)

    gate_all = fin[:, :, :, D : D + 1].reshape(SLOTS, 1).astype(F32)

    def down_part(shard, _):
        grads = grecv[shard].reshape(SLOTS, SH).astype(F32)
        scaled = (gate_all * grads).astype(BF)
        columns = pl.ds(pl.multiple_of(shard * SH, SH), SH)
        wd[:, columns] = dot(act[...], scaled, 0, 0).astype(BF)
        return 0

    lax.fori_loop(0, 8, down_part, 0)
    written = [local(wd, out_wd)]
    forward_back(2)

    def in_part(source, outgoing):
        def one(n, _):
            some = pl.ds(pl.multiple_of(n * 256, 256), 256)
            rows = fin[:, :, :, some].reshape(SLOTS, 256)
            outgoing[some, :] = dot(rows, source[...], 0, 0).astype(BF)
            return 0

        lax.fori_loop(0, 8, one, 0)

    in_part(dhg, wg)
    written.append(local(wg, out_wg))
    forward_back(3)
    in_part(dhu, wu)
    written.append(local(wu, out_wu))

    for step in range(4):
        for copy in r_two[step]:
            copy.wait_recv()
        for copy in t_two.get(step, []):
            copy.wait_recv()
    for copy in own_back:
        copy.wait()

    def gather_gates(d, total):
        rows = back[d // 4, d % 4, :, D:WIDE][:, 0:1].astype(F32)
        hot = pmat[pl.ds(pl.multiple_of(d * CAP, CAP), CAP), :].astype(F32)
        value = jnp.sum(hot * rows, axis=0, keepdims=True)
        wanted = (d * 8 + col).astype(F32)
        return total + jnp.where(slots[row] == wanted, value, 0.0)

    gsend[...] = lax.fori_loop(0, 16, gather_gates, jnp.zeros((8, TOK), F32))
    grecv_gates[col] = gsend[...]
    gate_sent = []
    for m in (0, 1, 3, 2):
        for f in range(2):
            if (m, f) != (0, 0):
                gate_sent.append(send(gsend, grecv_gates.at[col], xdev(m, f)))

    for copies in g_sent.values():
        copies.wait_send()

    def combine(shard):
        columns = pl.ds(pl.multiple_of(shard * SH, SH), SH)
        return dot(pmat[...], back[:, :, :, columns].reshape(SLOTS, SH), 0, 0)

    to_core = []
    for k in (1, 3, 2, 0):
        shard = at(k, x) * 2 + 1 - c
        gpack[shard, :, 0:2] = combine(shard).astype(BF).reshape(4, 2, CAP, SH)
        to_core.append(send(gpack.at[shard, :, 0:2], core_in.at[at(k, x)], xdev(0, 1)))
    to_x = []
    total = None
    for n, k in enumerate((1, 3, 2, 0)):
        shard = at(k, x) * 2 + c
        part = combine(shard)
        to_core[n].wait_recv()
        part = part + core_in[at(k, x)].reshape(TOK, SH).astype(F32)
        if k:
            gpack[shard, :, 0:2] = part.astype(BF).reshape(4, 2, CAP, SH)
            to_x.append(send(gpack.at[shard, :, 0:2], rs_in.at[x], xdev(k, 0)))
        else:
            total = part
    for n, k in enumerate(ORDER):
        to_x[n].wait_recv()
        total = total + rs_in[at(-k, x)].reshape(TOK, SH).astype(F32)
    out_in[...] = total.astype(BF)

    for copy in gate_sent:
        copy.wait_recv()
    out_gates[...] = jnp.sum(grecv_gates[...], axis=0)

    for copy in x_own + x_core + a_one + b_one + s_one + s_two + gate_sent + to_core + to_x:
        copy.wait_send()
    for k in (0,) + ORDER:
        for copy in a_two[k] + b_two[k]:
            copy.wait_send()
    for k in ORDER:
        for copy in p_two[k] + q_two[k]:
            copy.wait_send()
    for step in range(4):
        if step < 3:
            r_one[step].wait_send()
        for copy in t_one[step] + r_two[step] + t_two.get(step, []):
            copy.wait_send()
    for copy in written:
        copy.wait()


def body(inputs, grad_output, gates, expert_ids, owner, w_gate, w_up, w_down):
    vmem, anywhere = pl.BlockSpec(memory_space=pltpu.VMEM), pl.BlockSpec(memory_space=pl.ANY)
    scratch = [
        ((8, TOK, SH), BF),
        ((16, TOK, SH), BF),
        ((16, 8, TOK), F32),
        ((8, 4, 4, CAP, SH), BF),
        ((8, 4, 4, CAP, SH), BF),
        ((4, 4, CAP, WIDE), BF),
        ((4, 4, HALF, WIDE), BF),
        ((4, 4, HALF, WIDE), BF),
        ((4, 4, CAP, WIDE), BF),
        ((D, FF), BF),
        ((D, FF), BF),
        ((FF, D), BF),
        ((SLOTS, FF), F32),
        ((SLOTS, FF), BF),
        ((SLOTS, FF), BF),
        ((SLOTS, FF), BF),
        ((4, 4, HALF, WIDE), BF),
        ((4, 4, HALF, WIDE), BF),
        ((4, 4, CAP, WIDE), BF),
        ((SLOTS, TOK), BF),
        ((TOK, TOK), BF),
        ((128, TOK), F32),
        ((TOK, TOK), BF),
        ((4, 4, 2, CAP, SH), BF),
        ((4, 4, 2, CAP, SH), BF),
        ((8, TOK), F32),
        ((8, 8, TOK), F32),
    ]
    grad_inputs, grad_gates, grad_gate, grad_up, grad_down = pl.pallas_call(
        kernel,
        out_shape=[
            jax.ShapeDtypeStruct((TOK, SH), BF),
            jax.ShapeDtypeStruct((TOP, TOK), F32),
            jax.ShapeDtypeStruct((D, FF), BF),
            jax.ShapeDtypeStruct((D, FF), BF),
            jax.ShapeDtypeStruct((FF, D), BF),
        ],
        in_specs=[anywhere, anywhere, vmem, vmem, vmem, anywhere, anywhere, anywhere],
        out_specs=[vmem, vmem, anywhere, anywhere, anywhere],
        scratch_shapes=[pltpu.VMEM(shape, kind) for shape, kind in scratch]
        + [
            pltpu.SemaphoreType.DMA((SEMS,)),
            pltpu.SemaphoreType.DMA((SEMS,)),
            pltpu.SemaphoreType.DMA((SEMS // 4,)),
        ],
        compiler_params=pltpu.CompilerParams(
            collective_id=0, has_side_effects=True, vmem_limit_bytes=63 << 20
        ),
    )(
        inputs,
        grad_output,
        expert_ids.T,
        gates.T,
        owner.reshape(1, -1),
        w_gate[0],
        w_up[0],
        w_down[0],
    )
    return (
        grad_inputs,
        grad_gates.T.astype(BF),
        grad_gate[None],
        grad_up[None],
        grad_down[None],
    )


def solution(mesh):
    in_specs = (
        P("dp", "expert"),
        P("dp", "expert"),
        P("dp", None),
        P("dp", None),
        P(),
        P(("dp", "expert"), None, None),
        P(("dp", "expert"), None, None),
        P(("dp", "expert"), None, None),
    )
    out_specs = (
        P("dp", "expert"),
        P("dp", None),
        P(("dp", "expert"), None, None),
        P(("dp", "expert"), None, None),
        P(("dp", "expert"), None, None),
    )
    return jax.shard_map(body, mesh=mesh, in_specs=in_specs, out_specs=out_specs, check_vma=False)
```

profile of v0, /device:TPU:1, one launch (start us, length us, event | category | flops | bytes accessed | tf_op | source)
XLA Modules:
  0.0 183.4 jit_solution(11726344348041999338)
XLA Ops:
  0.6 171.2 %shard_map.119 = (bf16[512,256]{1,0:T(8,128)(2,1)}, f32[8,512]{1,0:T(8,128)}, bf16[2048,768]{1,0:T(8,128)(2,1)}, bf16[2048,768]{1,0:T(8,128)(2,1)}, bf16[768,2048]{1,0:T(8,128)(2,1)}) custom-call(bf16[512,256]{1,0:T(8,128)(2,1)} %inp.1, bf16[512,256]{1,0:T(8,128)(2,1)} %gro.1, s32[8,512]{1,0:T(8,128)} %bitcast.17, bf16[8,512]{1,0:T(8,128)(2,1)} %bitcast.18, ...), custom_call_target="tpu_custom_call" | custom-call | tf_op jit(solution)/shard_map/pallas_call | solution.py:452
  171.8 1.3 convert_bitcast_fusion
  173.1 1.7 copy.17
  174.8 0.0 copy-start.1
  174.8 3.9 %copy.18 = bf16[1,2048,768]{2,1,0:T(8,128)(2,1)} copy(bf16[1,2048,768]{2,1,0:T(8,128)(2,1)} %bitcast.13) | data formatting | bytes 6291456
  178.7 0.0 copy-done.1
  178.7 0.0 copy-start
  178.7 1.7 copy.19
  180.4 1.4 copy-done
  181.8 1.7 copy.20
Async XLA Ops:
  174.8 3.9 %copy-start.1 = (bf16[2048,768]{1,0:T(8,128)(2,1)S(1)}, bf16[2048,768]{1,0:T(8,128)(2,1)}, u32[]{:S(2)}) copy-start(bf16[2048,768]{1,0:T(8,128)(2,1)} %get-tuple-element.13) | copy-start | bytes 9437188
  178.7 3.0 %copy-start = (bf16[768,2048]{1,0:T(8,128)(2,1)S(1)}, bf16[768,2048]{1,0:T(8,128)(2,1)}, u32[]{:S(2)}) copy-start(bf16[768,2048]{1,0:T(8,128)(2,1)} %get-tuple-element.14) | copy-start | bytes 9437188
where the time goes:
time: 184 us; the launch traced here: 183 us
  Pallas kernels  171 us (93%)
  local copies, waits for them, and re-layouts  10.3 us (6%)
    pallas_call x1, Pallas kernels, body(): pl.pallas_call(kernel, out_shape=[jax.ShapeDtypeStruct((TOK, SH), BF), ja...  171 us
    unnamed x8, local copies, waits for them, and re-layouts  10.3 us

commit v1 on v0

--- a/solution.py
+++ b/solution.py
@@ -28,9 +28,9 @@
 
 def kernel(
     inp, gro, ids, gates, owner, wg_in, wu_in, wd_in,
-    out_in, out_gates, out_wg, out_wu, out_wd,
-    xin, ag, slots, gpack, grecv, pack, st1, st2, fin, wg, wu, wd, dz, act, dhg, dhu,
-    bst1, bst2, back, pmat, tri, rall, onehot, core_in, rs_in, gsend, grecv_gates,
+    out_in, out_gates, wg, wu, wd,
+    xin, ag, slots, gpack, grecv, pack, st1, st2, fin, dz, act, dhg, dhu,
+    bst1, bst2, back, pmat, pmat_t, tri, rall, onehot, core_in, rs_in, gsend, grecv_gates,
     send_sem, recv_sem, local_sem,
 ):
     row, col = lax.axis_index("dp"), lax.axis_index("expert")
@@ -66,6 +66,18 @@
         copy = pltpu.make_async_copy(src, dst, local_sem.at[n])
         copy.start()
         return copy
+
+    def arrive(label, copies):
+        for copy in copies:
+            copy.wait_recv()
+
+    def leave(label, copies):
+        for copy in copies:
+            copy.wait_send()
+
+    def done(label, copies):
+        for copy in copies:
+            copy.wait()
 
     weights = [local(wg_in, wg), local(wu_in, wu), local(wd_in, wd)]
     own_in, own_gro = local(inp, xin.at[col]), local(gro, ag.at[row])
@@ -109,64 +121,45 @@
         gate_col = jnp.sum(hot * gate_of[d : d + 1, :], axis=1, keepdims=True)
         pack[d // 4, d % 4, :, D:WIDE] = jnp.broadcast_to(gate_col, (CAP, 128)).astype(BF)
 
-    for copy in s_one:
-        copy.wait_recv()
+    arrive("slots", s_one)
     s_two = [
         send(slots.at[pl.ds(z * 4, 4)], slots.at[pl.ds(z * 4, 4)], zdev(k)) for k in ORDER
     ]
     for n, k in enumerate(ORDER):
-        x_own[n].wait_recv()
+        arrive("x_own", [x_own[n]])
         source = at(-k, x) * 2 + c
         x_core.append(send(xin.at[source], xin.at[source], xdev(0, 1)))
-        a_one[n].wait_recv()
+        arrive("a_one", [a_one[n]])
         source = z * 4 + at(-k, y)
         a_two[k] = [
             send(ag.at[source, lower], ag.at[source, lower], zdev(m)) for m in ORDER
         ]
-        b_one[n].wait_recv()
+        arrive("b_one", [b_one[n]])
         source = at(-k, z) * 4 + y
         b_two[k] = [
             send(ag.at[source, upper], ag.at[source, upper], ydev(m)) for m in ORDER
         ]
 
-    for copy in x_core:
-        copy.wait_recv()
-    own_in.wait()
-
-    def pack_inputs(shard, _):
-        rows = dot(pmat[...], xin[shard], 1, 0).astype(BF)
-        pack[:, :, :, pl.ds(pl.multiple_of(shard * SH, SH), SH)] = rows.reshape(4, 4, CAP, SH)
-        return 0
-
-    lax.fori_loop(0, 8, pack_inputs, 0)
-
-    first, second = pl.ds(0, HALF), pl.ds(HALF, HALF)
-    p_one = [send(pack.at[:, at(k, y), first], st1.at[y], ydev(k)) for k in ORDER]
-    q_one = [send(pack.at[at(k, z), :, second], st2.at[z], zdev(k)) for k in ORDER]
-    p_two = {0: [send(pack.at[at(k, z), y, first], fin.at[z, y, first], zdev(k)) for k in ORDER]}
-    q_two = {0: [send(pack.at[z, at(k, y), second], fin.at[z, y, second], ydev(k)) for k in ORDER]}
-    own_rows = [local(pack.at[z, y], fin.at[z, y])]
-
-    for copy in s_two:
-        copy.wait_recv()
-    own_gro.wait()
     near = iota((8, TOK), 0) + row.astype(F32) * 8.0
 
-    def find_members(r, _):
-        found = jnp.zeros((8, TOK), F32)
-        theirs = slots[r]
-        for k in range(TOP):
-            found += jnp.where(theirs[k : k + 1, :] == near, 1.0, 0.0)
-        rall[pl.ds(pl.multiple_of(r * 8, 8), 8), :] = found
-        return 0
-
-    lax.fori_loop(0, 16, find_members, 0)
-    rall[...] = dot(rall[...].astype(BF), tri[...], 1, 0) * rall[...]
+    def rank_members(group):
+        def one(step, _):
+            found = jnp.zeros((8, TOK), F32)
+            theirs = slots[group * 4 + step]
+            for k in range(TOP):
+                found += jnp.where(theirs[k : k + 1, :] == near, 1.0, 0.0)
+            rall[pl.ds(pl.multiple_of(step * 8, 8), 8), :] = found
+            return 0
+
+        lax.fori_loop(0, 4, one, 0)
+        rall[...] = dot(rall[...].astype(BF), tri[...], 1, 0) * rall[...]
 
     def pack_gradients(group):
+        rank_members(group)
+
         def one(step, _):
             r = group * 4 + step
-            ranks = rall[pl.ds(pl.multiple_of(r * 8, 8), 8), :]
+            ranks = rall[pl.ds(pl.multiple_of(step * 8, 8), 8), :]
             for e in range(8):
                 hot = jnp.where(ranks[e : e + 1, :] == place, 1.0, 0.0)
                 onehot[e * CAP : (e + 1) * CAP, :] = hot.astype(BF)
@@ -190,39 +183,53 @@
                         gpack.at[target, group], grecv.at[col, group], xdev(m, f)
                     )
 
-    for k in (0, 1, 3, 2):
-        if k == 0:
-            for copy in b_two[0]:
-                copy.wait_recv()
-        else:
-            b_seen = b_two[k]
-            for copy in b_seen:
-                copy.wait_recv()
-            n = ORDER.index(k)
-            for source in (0, 1, 3, 2):
-                a_two[source][n].wait_recv()
+    arrive("b_two", b_two[0])
+    own_gro.wait()
+    pack_gradients(z)
+    exchange_gradients(z, 0)
+
+    arrive("x_core", x_core)
+    own_in.wait()
+
+    def pack_inputs(shard, _):
+        rows = dot(pmat[...], xin[shard], 1, 0).astype(BF)
+        pack[:, :, :, pl.ds(pl.multiple_of(shard * SH, SH), SH)] = rows.reshape(4, 4, CAP, SH)
+        return 0
+
+    lax.fori_loop(0, 8, pack_inputs, 0)
+
+    first, second = pl.ds(0, HALF), pl.ds(HALF, HALF)
+    p_one = [send(pack.at[:, at(k, y), first], st1.at[y], ydev(k)) for k in ORDER]
+    q_one = [send(pack.at[at(k, z), :, second], st2.at[z], zdev(k)) for k in ORDER]
+    p_two = {0: [send(pack.at[at(k, z), y, first], fin.at[z, y, first], zdev(k)) for k in ORDER]}
+    q_two = {0: [send(pack.at[z, at(k, y), second], fin.at[z, y, second], ydev(k)) for k in ORDER]}
+    own_rows = [local(pack.at[z, y], fin.at[z, y])]
+
+    arrive("slots_two", s_two)
+    for n, k in enumerate(ORDER):
+        arrive("b_two", b_two[k])
+        arrive("a_two", [a_two[source][n] for source in (0, 1, 3, 2)])
         group = at(-k, z)
         pack_gradients(group)
         exchange_gradients(group, k)
 
     for n, k in enumerate(ORDER):
-        p_one[n].wait_recv()
+        arrive("p_one", [p_one[n]])
         source = at(-k, y)
         p_two[k] = [
             send(st1.at[source, at(m, z)], fin.at[z, source, first], zdev(m)) for m in ORDER
         ]
         own_rows.append(local(st1.at[source, z], fin.at[z, source, first]))
-        q_one[n].wait_recv()
+        arrive("q_one", [q_one[n]])
         source = at(-k, z)
         q_two[k] = [
             send(st2.at[source, at(m, y)], fin.at[source, y, second], ydev(m)) for m in ORDER
         ]
         own_rows.append(local(st2.at[source, y], fin.at[source, y, second]))
 
-    for copy in weights:
-        copy.wait()
-    for copy in own_grads:
-        copy.wait()
+    pmat_t[...] = pmat[...].T
+
+    done("weights", weights + own_grads)
 
     def add_dz(shard, start):
         columns = pl.ds(pl.multiple_of(shard * SH, SH), SH)
@@ -239,17 +246,13 @@
     for m in (0, 1, 3, 2):
         for f in range(2):
             if (m, f) != (0, 0):
-                for k in (0, 1, 3, 2):
-                    g_sent[k, m, f].wait_recv()
+                arrive("grads", [g_sent[k, m, f] for k in (0, 1, 3, 2)])
                 add_dz(at(-m, x) * 2 + (c + f) % 2, False)
 
-    for copy in p_one + q_one + p_two[0] + q_two[0]:
-        copy.wait_send()
+    leave("pack", p_one + q_one + p_two[0] + q_two[0])
     for k in (0,) + ORDER:
-        for copy in p_two[k] + q_two[k]:
-            copy.wait_recv()
-    for copy in own_rows:
-        copy.wait()
+        arrive("rows", p_two[k] + q_two[k])
+    done("own_rows", own_rows)
 
     def through_expert(group):
         rows = fin[group].reshape(256, WIDE)
@@ -283,7 +286,7 @@
 
     def forward_back(step):
         if step < 3:
-            r_one[step].wait_recv()
+            arrive("r_one", [r_one[step]])
             source = at(-1 - step, z)
             r_two[step] = [
                 send(bst1.at[source, at(m, y)], back.at[source, y, first], ydev(m)) for m in ORDER
@@ -291,7 +294,7 @@
             own_back.append(local(bst1.at[source, y], back.at[source, y, first]))
         target = at(1 + step, z)
         for n, k in enumerate(ORDER):
-            t_one[step][n].wait_recv()
+            arrive("t_one", [t_one[step][n]])
             source = at(-k, y)
             if step < 3:
                 t_two[step].append(
@@ -327,7 +330,6 @@
         return 0
 
     lax.fori_loop(0, 8, down_part, 0)
-    written = [local(wd, out_wd)]
     forward_back(2)
 
     def in_part(source, outgoing):
@@ -340,27 +342,23 @@
         lax.fori_loop(0, 8, one, 0)
 
     in_part(dhg, wg)
-    written.append(local(wg, out_wg))
     forward_back(3)
     in_part(dhu, wu)
-    written.append(local(wu, out_wu))
 
     for step in range(4):
-        for copy in r_two[step]:
-            copy.wait_recv()
-        for copy in t_two.get(step, []):
-            copy.wait_recv()
-    for copy in own_back:
-        copy.wait()
-
-    def gather_gates(d, total):
-        rows = back[d // 4, d % 4, :, D:WIDE][:, 0:1].astype(F32)
-        hot = pmat[pl.ds(pl.multiple_of(d * CAP, CAP), CAP), :].astype(F32)
-        value = jnp.sum(hot * rows, axis=0, keepdims=True)
-        wanted = (d * 8 + col).astype(F32)
-        return total + jnp.where(slots[row] == wanted, value, 0.0)
-
-    gsend[...] = lax.fori_loop(0, 16, gather_gates, jnp.zeros((8, TOK), F32))
+        arrive("r_two", r_two[step])
+        arrive("t_two", t_two.get(step, []))
+    done("own_back", own_back)
+
+    slot_no = lax.broadcasted_iota(jnp.int32, (SLOTS, 128), 0) // CAP
+    in_place = slot_no == lax.broadcasted_iota(jnp.int32, (SLOTS, 128), 1)
+    spread = jnp.where(in_place, back[:, :, :, D:WIDE].reshape(SLOTS, 128).astype(F32), 0.0)
+    values = dot(pmat_t[...], spread.astype(BF), 1, 0).T
+    total_gates = jnp.zeros((TOP, TOK), F32)
+    for d in range(16):
+        wanted = (col + d * 8).astype(F32)
+        total_gates += jnp.where(mine == wanted, values[d : d + 1, :], 0.0)
+    gsend[...] = total_gates
     grecv_gates[col] = gsend[...]
     gate_sent = []
     for m in (0, 1, 3, 2):
@@ -368,12 +366,11 @@
             if (m, f) != (0, 0):
                 gate_sent.append(send(gsend, grecv_gates.at[col], xdev(m, f)))
 
-    for copies in g_sent.values():
-        copies.wait_send()
+    leave("g_sent", g_sent.values())
 
     def combine(shard):
         columns = pl.ds(pl.multiple_of(shard * SH, SH), SH)
-        return dot(pmat[...], back[:, :, :, columns].reshape(SLOTS, SH), 0, 0)
+        return dot(pmat_t[...], back[:, :, :, columns].reshape(SLOTS, SH), 1, 0)
 
     to_core = []
     for k in (1, 3, 2, 0):
@@ -385,7 +382,7 @@
     for n, k in enumerate((1, 3, 2, 0)):
         shard = at(k, x) * 2 + c
         part = combine(shard)
-        to_core[n].wait_recv()
+        arrive("to_core", [to_core[n]])
         part = part + core_in[at(k, x)].reshape(TOK, SH).astype(F32)
         if k:
             gpack[shard, :, 0:2] = part.astype(BF).reshape(4, 2, CAP, SH)
@@ -393,28 +390,30 @@
         else:
             total = part
     for n, k in enumerate(ORDER):
-        to_x[n].wait_recv()
+        arrive("to_x", [to_x[n]])
         total = total + rs_in[at(-k, x)].reshape(TOK, SH).astype(F32)
     out_in[...] = total.astype(BF)
 
-    for copy in gate_sent:
-        copy.wait_recv()
-    out_gates[...] = jnp.sum(grecv_gates[...], axis=0)
-
-    for copy in x_own + x_core + a_one + b_one + s_one + s_two + gate_sent + to_core + to_x:
-        copy.wait_send()
+    arrive("gate_sent", gate_sent)
+    out_gates[...] = jnp.sum(grecv_gates[...], axis=0).astype(BF)
+
+    leave("first", x_own + x_core + a_one + b_one + s_one + s_two)
     for k in (0,) + ORDER:
-        for copy in a_two[k] + b_two[k]:
-            copy.wait_send()
+        leave("gather", a_two[k] + b_two[k])
     for k in ORDER:
-        for copy in p_two[k] + q_two[k]:
-            copy.wait_send()
+        leave("rows", p_two[k] + q_two[k])
     for step in range(4):
-        if step < 3:
-            r_one[step].wait_send()
-        for copy in t_one[step] + r_two[step] + t_two.get(step, []):
-            copy.wait_send()
-    for copy in written:
+        leave("back", t_one[step] + r_two[step] + t_two.get(step, []))
+    leave("back", r_one.values())
+    leave("sums", gate_sent + to_core + to_x)
+
+
+def write_out(*refs):
+    sem = refs[10]
+    copies = [pltpu.make_async_copy(refs[n], refs[5 + n], sem.at[n]) for n in range(5)]
+    for copy in copies:
+        copy.start()
+    for copy in copies:
         copy.wait()
 
 
@@ -430,9 +429,6 @@
         ((4, 4, HALF, WIDE), BF),
         ((4, 4, HALF, WIDE), BF),
         ((4, 4, CAP, WIDE), BF),
-        ((D, FF), BF),
-        ((D, FF), BF),
-        ((FF, D), BF),
         ((SLOTS, FF), F32),
         ((SLOTS, FF), BF),
         ((SLOTS, FF), BF),
@@ -441,25 +437,27 @@
         ((4, 4, HALF, WIDE), BF),
         ((4, 4, CAP, WIDE), BF),
         ((SLOTS, TOK), BF),
+        ((TOK, SLOTS), BF),
         ((TOK, TOK), BF),
-        ((128, TOK), F32),
+        ((32, TOK), F32),
         ((TOK, TOK), BF),
         ((4, 4, 2, CAP, SH), BF),
         ((4, 4, 2, CAP, SH), BF),
         ((8, TOK), F32),
         ((8, 8, TOK), F32),
     ]
-    grad_inputs, grad_gates, grad_gate, grad_up, grad_down = pl.pallas_call(
+    results = [
+        ((TOK, SH), BF),
+        ((TOP, TOK), BF),
+        ((D, FF), BF),
+        ((D, FF), BF),
+        ((FF, D), BF),
+    ]
+    held = pl.pallas_call(
         kernel,
-        out_shape=[
-            jax.ShapeDtypeStruct((TOK, SH), BF),
-            jax.ShapeDtypeStruct((TOP, TOK), F32),
-            jax.ShapeDtypeStruct((D, FF), BF),
-            jax.ShapeDtypeStruct((D, FF), BF),
-            jax.ShapeDtypeStruct((FF, D), BF),
-        ],
+        out_shape=[pltpu.VMEM(shape, kind) for shape, kind in results],
         in_specs=[anywhere, anywhere, vmem, vmem, vmem, anywhere, anywhere, anywhere],
-        out_specs=[vmem, vmem, anywhere, anywhere, anywhere],
+        out_specs=[vmem] * 5,
         scratch_shapes=[pltpu.VMEM(shape, kind) for shape, kind in scratch]
         + [
             pltpu.SemaphoreType.DMA((SEMS,)),
@@ -467,7 +465,7 @@
             pltpu.SemaphoreType.DMA((SEMS // 4,)),
         ],
         compiler_params=pltpu.CompilerParams(
-            collective_id=0, has_side_effects=True, vmem_limit_bytes=63 << 20
+            collective_id=0, has_side_effects=True, vmem_limit_bytes=53 << 20
         ),
     )(
         inputs,
@@ -479,9 +477,17 @@
         w_up[0],
         w_down[0],
     )
+    grad_inputs, grad_gates, grad_gate, grad_up, grad_down = pl.pallas_call(
+        write_out,
+        out_shape=[jax.ShapeDtypeStruct(shape, kind) for shape, kind in results],
+        in_specs=[vmem] * 5,
+        out_specs=[anywhere] * 5,
+        scratch_shapes=[pltpu.SemaphoreType.DMA((5,))],
+        compiler_params=pltpu.CompilerParams(vmem_limit_bytes=16 << 20),
+    )(*[pltpu.with_memory_space_constraint(array, pltpu.VMEM) for array in held])
     return (
         grad_inputs,
-        grad_gates.T.astype(BF),
+        grad_gates.T,
         grad_gate[None],
         grad_up[None],
         grad_down[None],

time: 184 us -> 175 us (0.951)
  local copies, waits for them, and re-layouts: 10.3 us -> 0 us
  Pallas kernels: 171 us -> 174 us
    unnamed x8 -> x0, local copies, waits for them, and re-layouts: 10.3 us -> none
    pallas_call x1 -> x2, Pallas kernels: 171 us -> 174 us  [the longest x1 170 us: body(): pl.pallas_call(kernel, out_shape=[pltpu.VMEM(shape, kind) for shape, kind...]
where the time goes in v1:
time: 175 us; the launch traced here: 174 us
  Pallas kernels  174 us (99%)
    pallas_call x1, Pallas kernels, body(): pl.pallas_call(kernel, out_shape=[pltpu.VMEM(shape, kind) for shape, kind...  170 us
    pallas_call x1, Pallas kernels, body(): pl.pallas_call(write_out, out_shape=[jax.ShapeDtypeStruct(shape, kind) fo...  3.87 us

profile of v1, /device:TPU:1, one launch (start us, length us, event | category | flops | bytes accessed | tf_op | source)
XLA Modules:
  0.0 174.4 jit_solution(1804235130018314510)
XLA Ops:
  0.6 169.8 %shard_map.119 = (bf16[512,256]{1,0:T(8,128)(2,1)S(1)}, bf16[8,512]{1,0:T(8,128)(2,1)S(1)}, bf16[2048,768]{1,0:T(8,128)(2,1)S(1)}, bf16[2048,768]{1,0:T(8,128)(2,1)S(1)}, bf16[768,2048]{1,0:T(8,128)(2,1)S(1)}) custom-call(bf16[512,256]{1,0:T(8,128)(2,1)} %inp.1, bf16[512,256]{1,0:T(8,128)(2,1)} %gro.1, s32[8,512]{1,0:T(8,128)} %bitcast.13, ...), custom_call_target="tpu_custom_call" | custom-call | tf_op jit(solution)/shard_map/pallas_call | solution.py:456
  170.4 3.9 %shard_map.120 = (bf16[512,256]{1,0:T(8,128)(2,1)}, bf16[8,512]{1,0:T(8,128)(2,1)}, bf16[2048,768]{1,0:T(8,128)(2,1)}, bf16[2048,768]{1,0:T(8,128)(2,1)}, bf16[768,2048]{1,0:T(8,128)(2,1)}) custom-call(bf16[512,256]{1,0:T(8,128)(2,1)S(1)} %get-tuple-element.15.refs_0_, bf16[8,512]{1,0:T(8,128)(2,1)S(1)} %get-tuple-element.16.refs_1_, ...), custom_call_target="tpu_custom_call" | custom-call | tf_op jit(solution)/shard_map/pallas_call | solution.py:480

commit v2 on v1

--- a/solution.py
+++ b/solution.py
@@ -10,7 +10,7 @@
 SH = 256
 WIDE = D + 128
 SLOTS = 1024
-SEMS = 160
+SEMS = 192
 BF, F32 = jnp.bfloat16, jnp.float32
 MESH = pl.DeviceIdType.MESH
 ORDER = (1, 3, 2)
@@ -29,8 +29,8 @@
 def kernel(
     inp, gro, ids, gates, owner, wg_in, wu_in, wd_in,
     out_in, out_gates, wg, wu, wd,
-    xin, ag, slots, gpack, grecv, pack, st1, st2, fin, dz, act, dhg, dhu,
-    bst1, bst2, back, pmat, pmat_t, tri, rall, onehot, core_in, rs_in, gsend, grecv_gates,
+    xin, ag, slots, gpack, grecv, pack, st1, st2, fin, dz, act, dhg, dhu, some_g, some_u,
+    bst1, bst2, back, pmat, pmat_t, tri, rall, onehot, gsend, grecv_gates,
     send_sem, recv_sem, local_sem,
 ):
     row, col = lax.axis_index("dp"), lax.axis_index("expert")
@@ -91,11 +91,42 @@
 
     x_own = [send(inp, xin.at[col], xdev(k, 0)) for k in ORDER]
     x_core = [send(inp, xin.at[col], xdev(0, 1))]
-    lower, upper = pl.ds(0, TOK // 2), pl.ds(TOK // 2, TOK // 2)
-    a_one = [send(gro.at[lower], ag.at[row, lower], ydev(k)) for k in ORDER]
-    b_one = [send(gro.at[upper], ag.at[row, upper], zdev(k)) for k in ORDER]
-    a_two = {0: [send(gro.at[lower], ag.at[row, lower], zdev(k)) for k in ORDER]}
-    b_two = {0: [send(gro.at[upper], ag.at[row, upper], ydev(k)) for k in ORDER]}
+    def half(path):
+        return pl.ds(path * 256, 256)
+
+    def quarter(path, n):
+        return pl.ds(path * 256 + n * 128, 128)
+
+    def along(path, stage, k):
+        return ydev(k) if path == stage - 1 else zdev(k)
+
+    def row_at(path, near, far):
+        if path == 0:
+            return at(far, z) * 4 + at(near, y)
+        return at(near, z) * 4 + at(far, y)
+
+    both = (1, -1)
+    one, two, one_on, two_on = {}, {}, {}, {}
+    for path in range(2):
+        for k in both:
+            one[path, k] = send(
+                gro.at[half(path)], ag.at[row, half(path)], along(path, 1, k)
+            )
+    for path in range(2):
+        for k in both:
+            two[path, 0, k] = send(
+                gro.at[half(path)], ag.at[row, half(path)], along(path, 2, k)
+            )
+
+    def pass_block(path, near):
+        here = ag.at[row_at(path, near, 0), half(path)]
+        for k in both:
+            two[path, near, k] = send(here, here, along(path, 2, k))
+
+    def pass_on(path, stage, near, k):
+        source = row_at(path, -k, 0) if stage == 1 else row_at(path, near, -k)
+        here = ag.at[source, quarter(path, 0 if k == 1 else 1)]
+        return send(here, here, along(path, stage, k))
 
     tri[...] = (iota((TOK, TOK), 0) <= iota((TOK, TOK), 1)).astype(BF)
     expert_no = lax.broadcasted_iota(jnp.int32, (128, TOK), 0)
@@ -125,29 +156,15 @@
     s_two = [
         send(slots.at[pl.ds(z * 4, 4)], slots.at[pl.ds(z * 4, 4)], zdev(k)) for k in ORDER
     ]
-    for n, k in enumerate(ORDER):
-        arrive("x_own", [x_own[n]])
-        source = at(-k, x) * 2 + c
-        x_core.append(send(xin.at[source], xin.at[source], xdev(0, 1)))
-        arrive("a_one", [a_one[n]])
-        source = z * 4 + at(-k, y)
-        a_two[k] = [
-            send(ag.at[source, lower], ag.at[source, lower], zdev(m)) for m in ORDER
-        ]
-        arrive("b_one", [b_one[n]])
-        source = at(-k, z) * 4 + y
-        b_two[k] = [
-            send(ag.at[source, upper], ag.at[source, upper], ydev(m)) for m in ORDER
-        ]
-
-    near = iota((8, TOK), 0) + row.astype(F32) * 8.0
+
+    neighbours = iota((8, TOK), 0) + row.astype(F32) * 8.0
 
     def rank_members(group):
         def one(step, _):
             found = jnp.zeros((8, TOK), F32)
             theirs = slots[group * 4 + step]
             for k in range(TOP):
-                found += jnp.where(theirs[k : k + 1, :] == near, 1.0, 0.0)
+                found += jnp.where(theirs[k : k + 1, :] == neighbours, 1.0, 0.0)
             rall[pl.ds(pl.multiple_of(step * 8, 8), 8), :] = found
             return 0
 
@@ -183,10 +200,35 @@
                         gpack.at[target, group], grecv.at[col, group], xdev(m, f)
                     )
 
-    arrive("b_two", b_two[0])
+    for path in range(2):
+        for k in both:
+            arrive("one", [one[path, k]])
+            one_on[path, k] = pass_on(path, 1, 0, k)
+            pass_block(path, -k)
+    for path in range(2):
+        for k in both:
+            arrive("two", [two[path, 0, k]])
+            two_on[path, 0, k] = pass_on(path, 2, 0, k)
+    for path in range(2):
+        arrive("one_on", [one_on[path, k] for k in both])
+        pass_block(path, 2)
+    for n, k in enumerate(ORDER):
+        arrive("x_own", [x_own[n]])
+        source = at(-k, x) * 2 + c
+        x_core.append(send(xin.at[source], xin.at[source], xdev(0, 1)))
+
+    def pass_far(near):
+        for path in range(2):
+            for k in both:
+                arrive("two", [two[path, near, k]])
+                two_on[path, near, k] = pass_on(path, 2, near, k)
+
+    arrive("two_on", [two_on[1, 0, k] for k in both])
     own_gro.wait()
     pack_gradients(z)
     exchange_gradients(z, 0)
+
+    pass_far(-1)
 
     arrive("x_core", x_core)
     own_in.wait()
@@ -199,16 +241,21 @@
     lax.fori_loop(0, 8, pack_inputs, 0)
 
     first, second = pl.ds(0, HALF), pl.ds(HALF, HALF)
-    p_one = [send(pack.at[:, at(k, y), first], st1.at[y], ydev(k)) for k in ORDER]
-    q_one = [send(pack.at[at(k, z), :, second], st2.at[z], zdev(k)) for k in ORDER]
     p_two = {0: [send(pack.at[at(k, z), y, first], fin.at[z, y, first], zdev(k)) for k in ORDER]}
     q_two = {0: [send(pack.at[z, at(k, y), second], fin.at[z, y, second], ydev(k)) for k in ORDER]}
     own_rows = [local(pack.at[z, y], fin.at[z, y])]
 
+    pass_far(1)
+    pass_far(2)
+    p_one = [send(pack.at[:, at(k, y), first], st1.at[y], ydev(k)) for k in ORDER]
+    q_one = [send(pack.at[at(k, z), :, second], st2.at[z], zdev(k)) for k in ORDER]
+
+    leave("x_core", x_core)
     arrive("slots_two", s_two)
-    for n, k in enumerate(ORDER):
-        arrive("b_two", b_two[k])
-        arrive("a_two", [a_two[source][n] for source in (0, 1, 3, 2)])
+    for k, near in zip(ORDER, (-1, 1, 2)):
+        arrive("two_on", [two_on[1, near, m] for m in both])
+        if k == 2:
+            arrive("two_on", [two_on[0, n, m] for n in (0, -1, 1, 2) for m in both])
         group = at(-k, z)
         pack_gradients(group)
         exchange_gradients(group, k)
@@ -235,9 +282,9 @@
         columns = pl.ds(pl.multiple_of(shard * SH, SH), SH)
 
         def chunk(n, _):
-            rows = pl.ds(pl.multiple_of(n * 256, 256), 256)
             part = dot(grecv[shard, n].reshape(256, SH), wd[:, columns], 1, 1)
-            dz[rows, :] = part if start else dz[rows, :] + part
+            part = part.reshape(4, CAP, FF)
+            dz[n] = part if start else dz[n] + part
             return 0
 
         lax.fori_loop(0, 4, chunk, 0)
@@ -250,75 +297,80 @@
                 add_dz(at(-m, x) * 2 + (c + f) % 2, False)
 
     leave("pack", p_one + q_one + p_two[0] + q_two[0])
-    for k in (0,) + ORDER:
-        arrive("rows", p_two[k] + q_two[k])
     done("own_rows", own_rows)
 
-    def through_expert(group):
-        rows = fin[group].reshape(256, WIDE)
+    def chunk_of(ref, zk, yk, width):
+        lower_rows = ref[zk, :, 0:HALF, 0:width].reshape(4 * HALF, width)
+        upper_rows = ref[:, yk, HALF:CAP, 0:width].reshape(4 * HALF, width)
+        return jnp.concatenate([lower_rows, upper_rows], axis=0)
+
+    def put_chunk(ref, zk, yk, columns, value):
+        width = value.shape[1]
+        ref[zk, :, 0:HALF, columns] = value[: 4 * HALF].reshape(4, HALF, width)
+        ref[:, yk, HALF:CAP, columns] = value[4 * HALF :].reshape(4, HALF, width)
+
+    def through_expert(zk, yk):
+        rows = chunk_of(fin, zk, yk, WIDE)
         gate_col = rows[:, D : D + 1].astype(F32)
         h1 = dot(rows[:, :D], wg[...], 1, 0)
         h2 = dot(rows[:, :D], wu[...], 1, 0)
-        here = pl.ds(pl.multiple_of(group * 256, 256), 256)
-        dz_here = dz[here, :]
+        dz_here = chunk_of(dz, zk, yk, FF)
         sigma = jax.nn.sigmoid(h1)
         silu = h1 * sigma
         slope = sigma * (1.0 + h1 * (1.0 - sigma))
         acted = (silu * h2).astype(BF)
-        act[here, :] = acted
+        every = pl.ds(0, FF)
+        put_chunk(act, zk, yk, every, acted)
         gate_grad = jnp.sum(acted.astype(F32) * dz_here, axis=1, keepdims=True)
-        pack[group, :, :, D:WIDE] = (
-            jnp.broadcast_to(gate_grad, (256, 128)).astype(BF).reshape(4, CAP, 128)
-        )
+        put_chunk(pack, zk, yk, pl.ds(D, 128), jnp.broadcast_to(gate_grad, (256, 128)).astype(BF))
         dfa = gate_col * dz_here
-        dhg[here, :] = (dfa * h2 * slope).astype(BF)
-        dhu[here, :] = (dfa * silu).astype(BF)
+        some_g[...] = (dfa * h2 * slope).astype(BF)
+        some_u[...] = (dfa * silu).astype(BF)
+        put_chunk(dhg, zk, yk, every, some_g[...])
+        put_chunk(dhu, zk, yk, every, some_u[...])
 
         def back_part(n, _):
             some = pl.ds(pl.multiple_of(n * 512, 512), 512)
-            part = dot(dhg[here, :], wg[some, :], 1, 1) + dot(dhu[here, :], wu[some, :], 1, 1)
-            pack[group, :, :, some] = part.astype(BF).reshape(4, CAP, 512)
+            part = dot(some_g[...], wg[some, :], 1, 1) + dot(some_u[...], wu[some, :], 1, 1)
+            put_chunk(pack, zk, yk, some, part.astype(BF))
             return 0
 
         lax.fori_loop(0, 4, back_part, 0)
 
     r_one, t_one, r_two, t_two, own_back = {}, {}, {}, {}, []
 
-    def forward_back(step):
-        if step < 3:
-            arrive("r_one", [r_one[step]])
-            source = at(-1 - step, z)
-            r_two[step] = [
-                send(bst1.at[source, at(m, y)], back.at[source, y, first], ydev(m)) for m in ORDER
-            ]
-            own_back.append(local(bst1.at[source, y], back.at[source, y, first]))
-        target = at(1 + step, z)
-        for n, k in enumerate(ORDER):
-            arrive("t_one", [t_one[step][n]])
-            source = at(-k, y)
-            if step < 3:
-                t_two[step].append(
-                    send(bst2.at[source, target], back.at[z, source, second], zdev(1 + step))
-                )
-            else:
-                own_back.append(local(bst2.at[source, z], back.at[z, source, second]))
-
-    for step in range(4):
-        group = at(1 + step, z)
-        through_expert(group)
-        if step < 3:
-            r_one[step] = send(pack.at[group, :, first], bst1.at[z], zdev(1 + step))
-            t_two[step] = [send(pack.at[group, y, second], back.at[z, y, second], zdev(1 + step))]
+    def forward_back(k):
+        arrive("r_one", [r_one[k]])
+        source = at(k, z)
+        r_two[k] = [
+            send(bst1.at[source, at(m, y)], back.at[source, y, first], ydev(m)) for m in ORDER
+        ]
+        own_back.append(local(bst1.at[source, y], back.at[source, y, first]))
+        arrive("t_one", [t_one[k]])
+        source = at(k, y)
+        t_two[k] = [
+            send(bst2.at[source, at(m, z)], back.at[z, source, second], zdev(m)) for m in ORDER
+        ]
+        own_back.append(local(bst2.at[source, z], back.at[z, source, second]))
+
+    for k in (0,) + ORDER:
+        zk, yk = at(-k, z), at(-k, y)
+        if k:
+            n = ORDER.index(k)
+            arrive("rows", [p_two[source][n] for source in (0, 1, 3, 2)])
+            arrive("rows", [q_two[source][n] for source in (0, 1, 3, 2)])
+        through_expert(zk, yk)
+        if k:
+            r_one[k] = send(pack.at[zk, :, first], bst1.at[z], zdev(-k))
+            t_one[k] = send(pack.at[:, yk, second], bst2.at[y], ydev(-k))
         else:
-            r_two[step] = [
+            r_two[0] = [
                 send(pack.at[z, at(m, y), first], back.at[z, y, first], ydev(m)) for m in ORDER
             ]
+            t_two[0] = [
+                send(pack.at[at(m, z), y, second], back.at[z, y, second], zdev(m)) for m in ORDER
+            ]
             own_back.append(local(pack.at[z, y], back.at[z, y]))
-        t_one[step] = [
-            send(pack.at[group, at(m, y), second], bst2.at[y, group], ydev(m)) for m in ORDER
-        ]
-        if step >= 2:
-            forward_back(step - 2)
 
     gate_all = fin[:, :, :, D : D + 1].reshape(SLOTS, 1).astype(F32)
 
@@ -326,29 +378,64 @@
         grads = grecv[shard].reshape(SLOTS, SH).astype(F32)
         scaled = (gate_all * grads).astype(BF)
         columns = pl.ds(pl.multiple_of(shard * SH, SH), SH)
-        wd[:, columns] = dot(act[...], scaled, 0, 0).astype(BF)
+        wd[:, columns] = dot(act[...].reshape(SLOTS, FF), scaled, 0, 0).astype(BF)
         return 0
 
-    lax.fori_loop(0, 8, down_part, 0)
-    forward_back(2)
+    lax.fori_loop(0, 4, down_part, 0)
+    forward_back(1)
+    lax.fori_loop(4, 8, down_part, 0)
+    forward_back(3)
 
     def in_part(source, outgoing):
         def one(n, _):
             some = pl.ds(pl.multiple_of(n * 256, 256), 256)
             rows = fin[:, :, :, some].reshape(SLOTS, 256)
-            outgoing[some, :] = dot(rows, source[...], 0, 0).astype(BF)
+            outgoing[some, :] = dot(rows, source[...].reshape(SLOTS, FF), 0, 0).astype(BF)
             return 0
 
         lax.fori_loop(0, 8, one, 0)
 
     in_part(dhg, wg)
-    forward_back(3)
+    forward_back(2)
     in_part(dhu, wu)
 
-    for step in range(4):
-        arrive("r_two", r_two[step])
-        arrive("t_two", t_two.get(step, []))
+    for k in (0,) + ORDER:
+        arrive("r_two", r_two[k])
+        arrive("t_two", t_two[k])
     done("own_back", own_back)
+
+    for sent in (one_on, two, two_on):
+        leave("gather", sent.values())
+
+    def combine(shard):
+        columns = pl.ds(pl.multiple_of(shard * SH, SH), SH)
+        return dot(pmat_t[...], back[:, :, :, columns].reshape(SLOTS, SH), 1, 0)
+
+    to_core, to_x = {}, {}
+
+    def for_other_core(k):
+        shard = at(k, x) * 2 + 1 - c
+        ag[shard] = combine(shard).astype(BF)
+        to_core[k] = send(ag.at[shard], xin.at[at(k, x)], xdev(0, 1))
+
+    def for_this_core(k):
+        shard = at(k, x) * 2 + c
+        part = combine(shard)
+        arrive("to_core", [to_core[k]])
+        part = part + xin[at(k, x)].astype(F32)
+        if k:
+            ag[shard] = part.astype(BF)
+            to_x[k] = send(ag.at[shard], xin.at[4 + x], xdev(k, 0))
+        return part
+
+    for_other_core(2)
+    for_other_core(1)
+    for_this_core(2)
+    for_other_core(3)
+    for_this_core(1)
+    for_other_core(0)
+    for_this_core(3)
+    total = for_this_core(0)
 
     slot_no = lax.broadcasted_iota(jnp.int32, (SLOTS, 128), 0) // CAP
     in_place = slot_no == lax.broadcasted_iota(jnp.int32, (SLOTS, 128), 1)
@@ -366,46 +453,24 @@
             if (m, f) != (0, 0):
                 gate_sent.append(send(gsend, grecv_gates.at[col], xdev(m, f)))
 
-    leave("g_sent", g_sent.values())
-
-    def combine(shard):
-        columns = pl.ds(pl.multiple_of(shard * SH, SH), SH)
-        return dot(pmat_t[...], back[:, :, :, columns].reshape(SLOTS, SH), 1, 0)
-
-    to_core = []
-    for k in (1, 3, 2, 0):
-        shard = at(k, x) * 2 + 1 - c
-        gpack[shard, :, 0:2] = combine(shard).astype(BF).reshape(4, 2, CAP, SH)
-        to_core.append(send(gpack.at[shard, :, 0:2], core_in.at[at(k, x)], xdev(0, 1)))
-    to_x = []
-    total = None
-    for n, k in enumerate((1, 3, 2, 0)):
-        shard = at(k, x) * 2 + c
-        part = combine(shard)
-        arrive("to_core", [to_core[n]])
-        part = part + core_in[at(k, x)].reshape(TOK, SH).astype(F32)
-        if k:
-            gpack[shard, :, 0:2] = part.astype(BF).reshape(4, 2, CAP, SH)
-            to_x.append(send(gpack.at[shard, :, 0:2], rs_in.at[x], xdev(k, 0)))
-        else:
-            total = part
-    for n, k in enumerate(ORDER):
-        arrive("to_x", [to_x[n]])
-        total = total + rs_in[at(-k, x)].reshape(TOK, SH).astype(F32)
+    for k in ORDER:
+        arrive("to_x", [to_x[k]])
+        total = total + xin[4 + at(-k, x)].astype(F32)
     out_in[...] = total.astype(BF)
 
     arrive("gate_sent", gate_sent)
     out_gates[...] = jnp.sum(grecv_gates[...], axis=0).astype(BF)
 
-    leave("first", x_own + x_core + a_one + b_one + s_one + s_two)
-    for k in (0,) + ORDER:
-        leave("gather", a_two[k] + b_two[k])
+    leave("first", x_own + s_one + s_two)
+    leave("gather", one.values())
+    leave("g_sent", g_sent.values())
     for k in ORDER:
         leave("rows", p_two[k] + q_two[k])
-    for step in range(4):
-        leave("back", t_one[step] + r_two[step] + t_two.get(step, []))
-    leave("back", r_one.values())
-    leave("sums", gate_sent + to_core + to_x)
+    for k in (0,) + ORDER:
+        leave("back", r_two[k] + t_two[k])
+    for k in ORDER:
+        leave("back", [r_one[k], t_one[k]])
+    leave("sums", gate_sent + list(to_core.values()) + list(to_x.values()))
 
 
 def write_out(*refs):
@@ -429,10 +494,12 @@
         ((4, 4, HALF, WIDE), BF),
         ((4, 4, HALF, WIDE), BF),
         ((4, 4, CAP, WIDE), BF),
-        ((SLOTS, FF), F32),
-        ((SLOTS, FF), BF),
-        ((SLOTS, FF), BF),
-        ((SLOTS, FF), BF),
+        ((4, 4, CAP, FF), F32),
+        ((4, 4, CAP, FF), BF),
+        ((4, 4, CAP, FF), BF),
+        ((4, 4, CAP, FF), BF),
+        ((256, FF), BF),
+        ((256, FF), BF),
         ((4, 4, HALF, WIDE), BF),
         ((4, 4, HALF, WIDE), BF),
         ((4, 4, CAP, WIDE), BF),
@@ -441,8 +508,6 @@
         ((TOK, TOK), BF),
         ((32, TOK), F32),
         ((TOK, TOK), BF),
-        ((4, 4, 2, CAP, SH), BF),
-        ((4, 4, 2, CAP, SH), BF),
         ((8, TOK), F32),
         ((8, 8, TOK), F32),
     ]

time: 175 us -> 167 us (0.954)
  Pallas kernels: 174 us -> 166 us
    pallas_call x1, Pallas kernels: 170 us -> 162 us  [body(): pl.pallas_call(kernel, out_shape=[pltpu.VMEM(shape, kind) for shape, kind...]
where the time goes in v2:
time: 167 us
  Pallas kernels  166 us (99%)
    pallas_call x1, Pallas kernels, body(): pl.pallas_call(kernel, out_shape=[pltpu.VMEM(shape, kind) for shape, kind...  162 us
    pallas_call x1, Pallas kernels, body(): pl.pallas_call(write_out, out_shape=[jax.ShapeDtypeStruct(shape, kind) fo...  3.87 us

profile of v2, /device:TPU:1, one launch (start us, length us, event | category | flops | bytes accessed | tf_op | source)
XLA Modules:
  0.0 166.8 jit_solution(13037144119753615912)
XLA Ops:
  0.6 162.2 %shard_map.119 = (bf16[512,256]{1,0:T(8,128)(2,1)S(1)}, bf16[8,512]{1,0:T(8,128)(2,1)S(1)}, bf16[2048,768]{1,0:T(8,128)(2,1)S(1)}, bf16[2048,768]{1,0:T(8,128)(2,1)S(1)}, bf16[768,2048]{1,0:T(8,128)(2,1)S(1)}) custom-call(bf16[512,256]{1,0:T(8,128)(2,1)} %inp.1, bf16[512,256]{1,0:T(8,128)(2,1)} %gro.1, s32[8,512]{1,0:T(8,128)} %bitcast.13, ...), custom_call_target="tpu_custom_call" | custom-call | tf_op jit(solution)/shard_map/pallas_call | solution.py:521
  162.8 3.9 %shard_map.120 = (bf16[512,256]{1,0:T(8,128)(2,1)}, bf16[8,512]{1,0:T(8,128)(2,1)}, bf16[2048,768]{1,0:T(8,128)(2,1)}, bf16[2048,768]{1,0:T(8,128)(2,1)}, bf16[768,2048]{1,0:T(8,128)(2,1)}) custom-call(bf16[512,256]{1,0:T(8,128)(2,1)S(1)} %get-tuple-element.15.refs_0_, bf16[8,512]{1,0:T(8,128)(2,1)S(1)} %get-tuple-element.16.refs_1_, ...), custom_call_target="tpu_custom_call" | custom-call | tf_op jit(solution)/shard_map/pallas_call | solution.py:545

commit v3 on v2

--- a/solution.py
+++ b/solution.py
@@ -10,7 +10,7 @@
 SH = 256
 WIDE = D + 128
 SLOTS = 1024
-SEMS = 192
+SEMS = 208
 BF, F32 = jnp.bfloat16, jnp.float32
 MESH = pl.DeviceIdType.MESH
 ORDER = (1, 3, 2)
@@ -332,26 +332,38 @@
         def back_part(n, _):
             some = pl.ds(pl.multiple_of(n * 512, 512), 512)
             part = dot(some_g[...], wg[some, :], 1, 1) + dot(some_u[...], wu[some, :], 1, 1)
-            put_chunk(pack, zk, yk, some, part.astype(BF))
+            part = part.astype(BF)
+            for h in range(2):
+                pieces = [part[:, m * 128 : m * 128 + 128] for m in (h, h + 2)]
+                columns = pl.ds(pl.multiple_of(h * 1024 + n * 256, 256), 256)
+                put_chunk(pack, zk, yk, columns, jnp.concatenate(pieces, axis=1))
             return 0
 
         lax.fori_loop(0, 4, back_part, 0)
 
-    r_one, t_one, r_two, t_two, own_back = {}, {}, {}, {}, []
-
-    def forward_back(k):
-        arrive("r_one", [r_one[k]])
+    r_one, t_one, r_two, t_two, own_back = {}, {}, {}, {}, ([], [])
+    lanes = (pl.ds(0, D // 2), pl.ds(D // 2, WIDE - D // 2))
+
+    def forward_back(k, h):
+        part = lanes[h]
+        arrive("r_one", [r_one[k, h]])
         source = at(k, z)
-        r_two[k] = [
-            send(bst1.at[source, at(m, y)], back.at[source, y, first], ydev(m)) for m in ORDER
+        r_two[k, h] = [
+            send(
+                bst1.at[source, at(m, y), :, part], back.at[source, y, first, part], ydev(m)
+            )
+            for m in ORDER
         ]
-        own_back.append(local(bst1.at[source, y], back.at[source, y, first]))
-        arrive("t_one", [t_one[k]])
+        own_back[h].append(local(bst1.at[source, y, :, part], back.at[source, y, first, part]))
+        arrive("t_one", [t_one[k, h]])
         source = at(k, y)
-        t_two[k] = [
-            send(bst2.at[source, at(m, z)], back.at[z, source, second], zdev(m)) for m in ORDER
+        t_two[k, h] = [
+            send(
+                bst2.at[source, at(m, z), :, part], back.at[z, source, second, part], zdev(m)
+            )
+            for m in ORDER
         ]
-        own_back.append(local(bst2.at[source, z], back.at[z, source, second]))
+        own_back[h].append(local(bst2.at[source, z, :, part], back.at[z, source, second, part]))
 
     for k in (0,) + ORDER:
         zk, yk = at(-k, z), at(-k, y)
@@ -360,17 +372,28 @@
             arrive("rows", [p_two[source][n] for source in (0, 1, 3, 2)])
             arrive("rows", [q_two[source][n] for source in (0, 1, 3, 2)])
         through_expert(zk, yk)
-        if k:
-            r_one[k] = send(pack.at[zk, :, first], bst1.at[z], zdev(-k))
-            t_one[k] = send(pack.at[:, yk, second], bst2.at[y], ydev(-k))
-        else:
-            r_two[0] = [
-                send(pack.at[z, at(m, y), first], back.at[z, y, first], ydev(m)) for m in ORDER
-            ]
-            t_two[0] = [
-                send(pack.at[at(m, z), y, second], back.at[z, y, second], zdev(m)) for m in ORDER
-            ]
-            own_back.append(local(pack.at[z, y], back.at[z, y]))
+        for h, part in enumerate(lanes):
+            if k:
+                r_one[k, h] = send(
+                    pack.at[zk, :, first, part], bst1.at[z, :, :, part], zdev(-k)
+                )
+                t_one[k, h] = send(
+                    pack.at[:, yk, second, part], bst2.at[y, :, :, part], ydev(-k)
+                )
+            else:
+                r_two[0, h] = [
+                    send(
+                        pack.at[z, at(m, y), first, part], back.at[z, y, first, part], ydev(m)
+                    )
+                    for m in ORDER
+                ]
+                t_two[0, h] = [
+                    send(
+                        pack.at[at(m, z), y, second, part], back.at[z, y, second, part], zdev(m)
+                    )
+                    for m in ORDER
+                ]
+                own_back[h].append(local(pack.at[z, y, :, part], back.at[z, y, :, part]))
 
     gate_all = fin[:, :, :, D : D + 1].reshape(SLOTS, 1).astype(F32)
 
@@ -382,9 +405,10 @@
         return 0
 
     lax.fori_loop(0, 4, down_part, 0)
-    forward_back(1)
+    forward_back(1, 0)
+    forward_back(1, 1)
     lax.fori_loop(4, 8, down_part, 0)
-    forward_back(3)
+    forward_back(3, 0)
 
     def in_part(source, outgoing):
         def one(n, _):
@@ -396,46 +420,48 @@
         lax.fori_loop(0, 8, one, 0)
 
     in_part(dhg, wg)
-    forward_back(2)
+    forward_back(2, 0)
+    forward_back(3, 1)
+    forward_back(2, 1)
     in_part(dhu, wu)
 
-    for k in (0,) + ORDER:
-        arrive("r_two", r_two[k])
-        arrive("t_two", t_two[k])
-    done("own_back", own_back)
-
-    for sent in (one_on, two, two_on):
-        leave("gather", sent.values())
-
-    def combine(shard):
-        columns = pl.ds(pl.multiple_of(shard * SH, SH), SH)
-        return dot(pmat_t[...], back[:, :, :, columns].reshape(SLOTS, SH), 1, 0)
-
-    to_core, to_x = {}, {}
-
-    def for_other_core(k):
-        shard = at(k, x) * 2 + 1 - c
-        ag[shard] = combine(shard).astype(BF)
-        to_core[k] = send(ag.at[shard], xin.at[at(k, x)], xdev(0, 1))
-
-    def for_this_core(k):
-        shard = at(k, x) * 2 + c
-        part = combine(shard)
-        arrive("to_core", [to_core[k]])
-        part = part + xin[at(k, x)].astype(F32)
+    leave("gather", list(one_on.values()) + list(two.values()) + list(two_on.values()))
+    to_core, to_x, own_sum = {}, {}, {}
+    sums_at = (pl.ds(0, 128), pl.ds(128, 128))
+
+    def sum_pair(k, h):
+        columns = pl.ds(pl.multiple_of(h * 1024 + at(k, x) * 256, 256), 256)
+        pair = dot(pmat_t[...], back[:, :, :, columns].reshape(SLOTS, 256), 1, 0)
+        ours = jnp.where(c == 0, pair[:, :128], pair[:, 128:])
+        theirs = jnp.where(c == 0, pair[:, 128:], pair[:, :128])
+        for n in range(2):
+            dz[k, :, :, n * 128 : n * 128 + 128] = ours[n * 256 : n * 256 + 256].reshape(4, CAP, 128)
+        ag[k, :, sums_at[h]] = theirs.astype(BF)
+        to_core[k, h] = send(ag.at[k, :, sums_at[h]], xin.at[at(k, x), :, sums_at[h]], xdev(0, 1))
+
+    def send_sum(k, h):
+        arrive("to_core", [to_core[k, h]])
+        ours = [dz[k, :, :, n * 128 : n * 128 + 128].reshape(256, 128) for n in range(2)]
+        part = jnp.concatenate(ours, axis=0) + xin[at(k, x), :, sums_at[h]].astype(F32)
         if k:
-            ag[shard] = part.astype(BF)
-            to_x[k] = send(ag.at[shard], xin.at[4 + x], xdev(k, 0))
-        return part
-
-    for_other_core(2)
-    for_other_core(1)
-    for_this_core(2)
-    for_other_core(3)
-    for_this_core(1)
-    for_other_core(0)
-    for_this_core(3)
-    total = for_this_core(0)
+            ag[4 + k, :, sums_at[h]] = part.astype(BF)
+            to_x[k, h] = send(ag.at[4 + k, :, sums_at[h]], xin.at[4 + x, :, sums_at[h]], xdev(k, 0))
+        else:
+            own_sum[h] = part
+
+    for h in range(2):
+        for k in (0,) + ORDER:
+            arrive("r_two", r_two[k, h])
+            arrive("t_two", t_two[k, h])
+        done("own_back", own_back[h])
+        sum_pair(2, h)
+        sum_pair(1, h)
+        send_sum(2, h)
+        sum_pair(3, h)
+        send_sum(1, h)
+        sum_pair(0, h)
+        send_sum(3, h)
+        send_sum(0, h)
 
     slot_no = lax.broadcasted_iota(jnp.int32, (SLOTS, 128), 0) // CAP
     in_place = slot_no == lax.broadcasted_iota(jnp.int32, (SLOTS, 128), 1)
@@ -453,10 +479,12 @@
             if (m, f) != (0, 0):
                 gate_sent.append(send(gsend, grecv_gates.at[col], xdev(m, f)))
 
-    for k in ORDER:
-        arrive("to_x", [to_x[k]])
-        total = total + xin[4 + at(-k, x)].astype(F32)
-    out_in[...] = total.astype(BF)
+    for h in range(2):
+        total = own_sum[h]
+        for k in ORDER:
+            arrive("to_x", [to_x[k, h]])
+            total = total + xin[4 + at(-k, x), :, sums_at[h]].astype(F32)
+        out_in[:, sums_at[h]] = total.astype(BF)
 
     arrive("gate_sent", gate_sent)
     out_gates[...] = jnp.sum(grecv_gates[...], axis=0).astype(BF)
@@ -466,10 +494,11 @@
     leave("g_sent", g_sent.values())
     for k in ORDER:
         leave("rows", p_two[k] + q_two[k])
-    for k in (0,) + ORDER:
-        leave("back", r_two[k] + t_two[k])
-    for k in ORDER:
-        leave("back", [r_one[k], t_one[k]])
+    for h in range(2):
+        for k in (0,) + ORDER:
+            leave("back", r_two[k, h] + t_two[k, h])
+        for k in ORDER:
+            leave("back", [r_one[k, h], t_one[k, h]])
     leave("sums", gate_sent + list(to_core.values()) + list(to_x.values()))
 
 

time: 167 us -> 162 us (0.970)
  Pallas kernels: 166 us -> 161 us
    pallas_call x1, Pallas kernels: 162 us -> 157 us  [body(): pl.pallas_call(kernel, out_shape=[pltpu.VMEM(shape, kind) for shape, kind...]
where the time goes in v3:
time: 162 us
  Pallas kernels  161 us (99%)
    pallas_call x1, Pallas kernels, body(): pl.pallas_call(kernel, out_shape=[pltpu.VMEM(shape, kind) for shape, kind...  157 us
    pallas_call x1, Pallas kernels, body(): pl.pallas_call(write_out, out_shape=[jax.ShapeDtypeStruct(shape, kind) fo...  3.87 us

profile of v3, /device:TPU:1, one launch (start us, length us, event | category | flops | bytes accessed | tf_op | source)
XLA Modules:
  0.0 161.6 jit_solution(1694464678975826786)
XLA Ops:
  0.6 156.9 %shard_map.119 = (bf16[512,256]{1,0:T(8,128)(2,1)S(1)}, bf16[8,512]{1,0:T(8,128)(2,1)S(1)}, bf16[2048,768]{1,0:T(8,128)(2,1)S(1)}, bf16[2048,768]{1,0:T(8,128)(2,1)S(1)}, bf16[768,2048]{1,0:T(8,128)(2,1)S(1)}) custom-call(bf16[512,256]{1,0:T(8,128)(2,1)} %inp.1, bf16[512,256]{1,0:T(8,128)(2,1)} %gro.1, s32[8,512]{1,0:T(8,128)} %bitcast.13, ...), custom_call_target="tpu_custom_call" | custom-call | tf_op jit(solution)/shard_map/pallas_call | solution.py:550
  157.6 3.9 %shard_map.120 = (bf16[512,256]{1,0:T(8,128)(2,1)}, bf16[8,512]{1,0:T(8,128)(2,1)}, bf16[2048,768]{1,0:T(8,128)(2,1)}, bf16[2048,768]{1,0:T(8,128)(2,1)}, bf16[768,2048]{1,0:T(8,128)(2,1)}) custom-call(bf16[512,256]{1,0:T(8,128)(2,1)S(1)} %get-tuple-element.15.refs_0_, bf16[8,512]{1,0:T(8,128)(2,1)S(1)} %get-tuple-element.16.refs_1_, ...), custom_call_target="tpu_custom_call" | custom-call | tf_op jit(solution)/shard_map/pallas_call | solution.py:574

commit v4 on v3

--- a/solution.py
+++ b/solution.py
@@ -406,9 +406,9 @@
 
     lax.fori_loop(0, 4, down_part, 0)
     forward_back(1, 0)
-    forward_back(1, 1)
     lax.fori_loop(4, 8, down_part, 0)
     forward_back(3, 0)
+    forward_back(1, 1)
 
     def in_part(source, outgoing):
         def one(n, _):

time: 162 us -> 162 us (level)
  no operation moved by 1% of the time
where the time goes in v4:
time: 162 us
  Pallas kernels  161 us (99%)
    pallas_call x1, Pallas kernels, body(): pl.pallas_call(kernel, out_shape=[pltpu.VMEM(shape, kind) for shape, kind...  157 us
    pallas_call x1, Pallas kernels, body(): pl.pallas_call(write_out, out_shape=[jax.ShapeDtypeStruct(shape, kind) fo...  3.87 us

profile of v4, /device:TPU:1, one launch (start us, length us, event | category | flops | bytes accessed | tf_op | source)
XLA Modules:
  0.0 161.6 jit_solution(17957940402756708520)
XLA Ops:
  0.6 156.9 %shard_map.119 = (bf16[512,256]{1,0:T(8,128)(2,1)S(1)}, bf16[8,512]{1,0:T(8,128)(2,1)S(1)}, bf16[2048,768]{1,0:T(8,128)(2,1)S(1)}, bf16[2048,768]{1,0:T(8,128)(2,1)S(1)}, bf16[768,2048]{1,0:T(8,128)(2,1)S(1)}) custom-call(bf16[512,256]{1,0:T(8,128)(2,1)} %inp.1, bf16[512,256]{1,0:T(8,128)(2,1)} %gro.1, s32[8,512]{1,0:T(8,128)} %bitcast.13, ...), custom_call_target="tpu_custom_call" | custom-call | tf_op jit(solution)/shard_map/pallas_call | solution.py:550
  157.6 3.9 %shard_map.120 = (bf16[512,256]{1,0:T(8,128)(2,1)}, bf16[8,512]{1,0:T(8,128)(2,1)}, bf16[2048,768]{1,0:T(8,128)(2,1)}, bf16[2048,768]{1,0:T(8,128)(2,1)}, bf16[768,2048]{1,0:T(8,128)(2,1)}) custom-call(bf16[512,256]{1,0:T(8,128)(2,1)S(1)} %get-tuple-element.15.refs_0_, bf16[8,512]{1,0:T(8,128)(2,1)S(1)} %get-tuple-element.16.refs_1_, ...), custom_call_target="tpu_custom_call" | custom-call | tf_op jit(solution)/shard_map/pallas_call | solution.py:574
